TPU v7x, 512 devices: a whole 4x4x16 slice. The times are simulated.
512 devices in a mesh: segment: 16 (over x, y), width: 32 (over z, core).
Axes of the slice: x: 4, y: 4, z: 16, core: 2. Of those that a mesh axis runs over, the one named last changes fastest.
Arguments:
- samples: bfloat16 [32, 65536], P(None, 'width'), may hold values from -6 to 6
- occupancy: int32 [16, 512, 4], P('segment'), may hold values from 0 to 511, as said below
- weights: bfloat16 [16, 512, 4, 128, 128], P('segment', 'width'), may hold values from -0.375 to 0.375
- biases: float32 [16, 65536], P('segment', 'width'), may hold values from -3 to 3
Outputs:
- final: bfloat16 [32, 65536], P('segment', 'width')
Inputs may be any that keep to these rules, and one draw needn't show every extreme that they name: `occupancy`: for each layer and width index d, the 16 column blocks d*16 to (d+1)*16 - 1 each name 4 different row blocks; together they name 32 different row blocks, each by exactly 2 of them, at most 2 in any one range e*16 to (e+1)*16 - 1, and exactly 2 in some ranges.
All inputs are finite; a program needn't handle non-finite values.
Results may differ from a plain program's by a relative error of at most 0.025.
Values may be sent and summed in bfloat16 or wider, within the bound.
A program may use at most 64 MiB of HBM per device.

v0:
```python
import jax
import jax.numpy as jnp
from jax import lax
from jax.sharding import PartitionSpec as P

MICRO = 4
BATCH = 8


clip_level = 4.0


def shifted(array, axis, by):
    length = lax.axis_size(axis)
    pairs = [(i, i + by) for i in range(length) if 0 <= i + by < length]
    return lax.ppermute(array, axis, pairs)


def spread(block, axis, holder):
    block = jnp.where(lax.axis_index(axis) == holder, block, jnp.zeros_like(block))
    return lax.psum(block, axis)


def per_device(samples, occupancy, weights, biases):
    segments = lax.axis_size("segment")
    shards = lax.axis_size("width")
    segment = lax.axis_index("segment")
    shard = lax.axis_index("width")
    occ = occupancy[0]
    blocks_w = weights[0]
    bias = biases[0]
    owned = blocks_w.shape[0]
    per_col = blocks_w.shape[1]
    order = blocks_w.shape[2]
    columns = samples.shape[1]
    capacity = 4 * owned // shards
    mine_occ = lax.dynamic_slice_in_dim(occ, shard * owned, owned, 0)
    requests = owned * per_col
    block_ids = jnp.arange(owned, dtype=jnp.int32)
    slots = 2 * capacity
    occ_all = occ.reshape(shards, requests)
    is_mine = (occ_all // owned == shard).astype(jnp.int32)
    rank_req = jnp.cumsum(is_mine, axis=1) - 1
    located = occ_all % owned
    slot_ids = jnp.arange(slots, dtype=jnp.int32)
    hit = (is_mine[:, None, :] == 1) & (rank_req[:, None, :] == slot_ids[None, :, None])
    select = jnp.sum(
        (hit[:, :, :, None] & (located[:, None, :, None] == block_ids[None, None, None, :])).astype(
            jnp.int32
        ),
        axis=2,
    ).astype(jnp.bfloat16)
    source = mine_occ.reshape(-1) // owned
    positions = jnp.arange(requests, dtype=jnp.int32)
    earlier = (source[None, :] == source[:, None]) & (positions[None, :] < positions[:, None])
    rank_own = jnp.sum(earlier.astype(jnp.int32), axis=1)
    flat_index = (source * slots + rank_own).reshape(owned, per_col)
    bias_blocks = bias.reshape(owned, order)

    def layer(inputs):
        pieces = inputs.reshape(BATCH, owned, order)
        outgoing = jnp.einsum(
            "drj,bjn->drbn", select, pieces, preferred_element_type=jnp.float32
        ).astype(jnp.bfloat16)
        arrived = lax.all_to_all(outgoing, "width", split_axis=0, concat_axis=0, tiled=True)
        picked = arrived.reshape(shards * slots, BATCH, order)[flat_index]
        pre = jnp.einsum("ckbi,ckio->bco", picked, blocks_w, preferred_element_type=jnp.float32)
        pre = pre + bias_blocks[None, :, :]
        return jnp.clip(pre, 0.0, clip_level).astype(jnp.bfloat16).reshape(BATCH, owned * order)

    def advance(step, state):
        carried, finished = state
        start = jnp.minimum(step, MICRO - 1) * BATCH
        fresh = lax.dynamic_slice_in_dim(samples, start, BATCH, 0)
        inputs = jnp.where(segment == 0, fresh, carried)
        result = layer(inputs)
        slot = jnp.clip(step - (segments - 1), 0, MICRO - 1)
        keep = (segment == segments - 1) & (step >= segments - 1)
        previous = lax.dynamic_slice_in_dim(finished, slot * BATCH, BATCH, 0)
        finished = lax.dynamic_update_slice_in_dim(
            finished, jnp.where(keep, result, previous), slot * BATCH, 0
        )
        carried = shifted(result, "segment", 1)
        return (carried, finished)

    carried0 = jnp.zeros((BATCH, columns), jnp.bfloat16)
    finished0 = jnp.zeros((MICRO * BATCH, columns), jnp.bfloat16)
    carried, finished = lax.fori_loop(0, MICRO + segments - 1, advance, (carried0, finished0))
    whole = spread(finished, "segment", segments - 1)
    share = whole.shape[0] // segments
    return lax.dynamic_slice_in_dim(whole, segment * share, share, 0)


def solution(mesh):
    in_specs = (
        P(None, "width"),
        P("segment", None, None),
        P("segment", "width", None, None, None),
        P("segment", "width"),
    )
    out_specs = P("segment", "width")
    return jax.shard_map(
        per_device, mesh=mesh, in_specs=in_specs, out_specs=out_specs, check_vma=False
    )
```

profile of v0, /device:TPU:6, one launch (start us, length us, event | category | flops | bytes accessed | tf_op | source)
XLA Modules:
  0.0 850.8 jit_solution(16344589100312160793)
XLA Ops:
  12.4 728.2 %while.17 = (s32[]{:T(128)}, bf16[8,2048]{1,0:T(8,128)(2,1)S(1)}, bf16[32,2048]{1,0:T(8,128)(2,1)S(1)}, pred[]{:T(512)}, bf16[32,2048]{1,0:T(8,128)(2,1)}, /*ind...) while((s32[]{:T(128)}, bf16[8,2048]{1,0:T(8,128)(2,1)S(1)}, ...), condition=%wide.region_4.5_spmd, body=%wide.region_3.4_spmd.sunk | while | flops 21185744 | bytes 13388223 | solution.py:88
  14.5 15.5 %all-to-all-start = ((bf16[32,4,8,128]{3,1,2,0:T(4,128)(2,1)}), bf16[32,4,8,128]{3,1,2,0:T(4,128)(2,1)S(1)}, u32[]{:S(2)}, u32[]{:S(2)}) async-start(bf16[32,4,8,128]{3,1,2,0:T(4,128)(2,1)} %copy.42), calls=%async_computation | async-start | bytes 524288 | tf_op jit(solution)/shard_map/while/body/eval_jaxpr/all_to_all | solution.py:65
  30.2 22.5 %all-to-all-done = bf16[32,4,8,128]{3,1,2,0:T(4,128)(2,1)S(1)} async-done(((bf16[32,4,8,128]{3,1,2,0:T(4,128)(2,1)}), bf16[32,4,8,128]{3,1,2,0:T(4,128)(2,1)S(1)}, u32[]{:S(2)}, u32[]{:S(2)}) %all-to-all-start) | async-done | bytes 262176 | tf_op jit(solution)/shard_map/while/body/eval_jaxpr/all_to_all | solution.py:65
  67.9 22.6 %all-to-all-done = bf16[32,4,8,128]{3,1,2,0:T(4,128)(2,1)S(1)} async-done(((bf16[32,4,8,128]{3,1,2,0:T(4,128)(2,1)}), bf16[32,4,8,128]{3,1,2,0:T(4,128)(2,1)S(1)}, u32[]{:S(2)}, u32[]{:S(2)}) %all-to-all-start) | async-done | bytes 262176 | tf_op jit(solution)/shard_map/while/body/eval_jaxpr/all_to_all | solution.py:65
  93.5 6.0 collective-permute-done
  105.6 22.6 %all-to-all-done = bf16[32,4,8,128]{3,1,2,0:T(4,128)(2,1)S(1)} async-done(((bf16[32,4,8,128]{3,1,2,0:T(4,128)(2,1)}), bf16[32,4,8,128]{3,1,2,0:T(4,128)(2,1)S(1)}, u32[]{:S(2)}, u32[]{:S(2)}) %all-to-all-start) | async-done | bytes 262176 | tf_op jit(solution)/shard_map/while/body/eval_jaxpr/all_to_all | solution.py:65
  131.2 6.0 collective-permute-done
  143.3 22.6 %all-to-all-done = bf16[32,4,8,128]{3,1,2,0:T(4,128)(2,1)S(1)} async-done(((bf16[32,4,8,128]{3,1,2,0:T(4,128)(2,1)}), bf16[32,4,8,128]{3,1,2,0:T(4,128)(2,1)S(1)}, u32[]{:S(2)}, u32[]{:S(2)}) %all-to-all-start) | async-done | bytes 262176 | tf_op jit(solution)/shard_map/while/body/eval_jaxpr/all_to_all | solution.py:65
  181.0 22.6 %all-to-all-done = bf16[32,4,8,128]{3,1,2,0:T(4,128)(2,1)S(1)} async-done(((bf16[32,4,8,128]{3,1,2,0:T(4,128)(2,1)}), bf16[32,4,8,128]{3,1,2,0:T(4,128)(2,1)S(1)}, u32[]{:S(2)}, u32[]{:S(2)}) %all-to-all-start) | async-done | bytes 262176 | tf_op jit(solution)/shard_map/while/body/eval_jaxpr/all_to_all | solution.py:65
  206.6 6.0 collective-permute-done
  218.7 22.6 %all-to-all-done = bf16[32,4,8,128]{3,1,2,0:T(4,128)(2,1)S(1)} async-done(((bf16[32,4,8,128]{3,1,2,0:T(4,128)(2,1)}), bf16[32,4,8,128]{3,1,2,0:T(4,128)(2,1)S(1)}, u32[]{:S(2)}, u32[]{:S(2)}) %all-to-all-start) | async-done | bytes 262176 | tf_op jit(solution)/shard_map/while/body/eval_jaxpr/all_to_all | solution.py:65
  256.4 22.6 %all-to-all-done = bf16[32,4,8,128]{3,1,2,0:T(4,128)(2,1)S(1)} async-done(((bf16[32,4,8,128]{3,1,2,0:T(4,128)(2,1)}), bf16[32,4,8,128]{3,1,2,0:T(4,128)(2,1)S(1)}, u32[]{:S(2)}, u32[]{:S(2)}) %all-to-all-start) | async-done | bytes 262176 | tf_op jit(solution)/shard_map/while/body/eval_jaxpr/all_to_all | solution.py:65
  282.0 6.0 collective-permute-done
  294.1 22.6 %all-to-all-done = bf16[32,4,8,128]{3,1,2,0:T(4,128)(2,1)S(1)} async-done(((bf16[32,4,8,128]{3,1,2,0:T(4,128)(2,1)}), bf16[32,4,8,128]{3,1,2,0:T(4,128)(2,1)S(1)}, u32[]{:S(2)}, u32[]{:S(2)}) %all-to-all-start) | async-done | bytes 262176 | tf_op jit(solution)/shard_map/while/body/eval_jaxpr/all_to_all | solution.py:65
  319.7 6.0 collective-permute-done
  331.9 22.6 %all-to-all-done = bf16[32,4,8,128]{3,1,2,0:T(4,128)(2,1)S(1)} async-done(((bf16[32,4,8,128]{3,1,2,0:T(4,128)(2,1)}), bf16[32,4,8,128]{3,1,2,0:T(4,128)(2,1)S(1)}, u32[]{:S(2)}, u32[]{:S(2)}) %all-to-all-start) | async-done | bytes 262176 | tf_op jit(solution)/shard_map/while/body/eval_jaxpr/all_to_all | solution.py:65
  369.6 22.6 %all-to-all-done = bf16[32,4,8,128]{3,1,2,0:T(4,128)(2,1)S(1)} async-done(((bf16[32,4,8,128]{3,1,2,0:T(4,128)(2,1)}), bf16[32,4,8,128]{3,1,2,0:T(4,128)(2,1)S(1)}, u32[]{:S(2)}, u32[]{:S(2)}) %all-to-all-start) | async-done | bytes 262176 | tf_op jit(solution)/shard_map/while/body/eval_jaxpr/all_to_all | solution.py:65
  407.3 22.6 %all-to-all-done = bf16[32,4,8,128]{3,1,2,0:T(4,128)(2,1)S(1)} async-done(((bf16[32,4,8,128]{3,1,2,0:T(4,128)(2,1)}), bf16[32,4,8,128]{3,1,2,0:T(4,128)(2,1)S(1)}, u32[]{:S(2)}, u32[]{:S(2)}) %all-to-all-start) | async-done | bytes 262176 | tf_op jit(solution)/shard_map/while/body/eval_jaxpr/all_to_all | solution.py:65
  432.9 6.0 collective-permute-done
  445.0 22.6 %all-to-all-done = bf16[32,4,8,128]{3,1,2,0:T(4,128)(2,1)S(1)} async-done(((bf16[32,4,8,128]{3,1,2,0:T(4,128)(2,1)}), bf16[32,4,8,128]{3,1,2,0:T(4,128)(2,1)S(1)}, u32[]{:S(2)}, u32[]{:S(2)}) %all-to-all-start) | async-done | bytes 262176 | tf_op jit(solution)/shard_map/while/body/eval_jaxpr/all_to_all | solution.py:65
  470.6 6.0 collective-permute-done
  482.7 22.6 %all-to-all-done = bf16[32,4,8,128]{3,1,2,0:T(4,128)(2,1)S(1)} async-done(((bf16[32,4,8,128]{3,1,2,0:T(4,128)(2,1)}), bf16[32,4,8,128]{3,1,2,0:T(4,128)(2,1)S(1)}, u32[]{:S(2)}, u32[]{:S(2)}) %all-to-all-start) | async-done | bytes 262176 | tf_op jit(solution)/shard_map/while/body/eval_jaxpr/all_to_all | solution.py:65
  520.4 22.6 %all-to-all-done = bf16[32,4,8,128]{3,1,2,0:T(4,128)(2,1)S(1)} async-done(((bf16[32,4,8,128]{3,1,2,0:T(4,128)(2,1)}), bf16[32,4,8,128]{3,1,2,0:T(4,128)(2,1)S(1)}, u32[]{:S(2)}, u32[]{:S(2)}) %all-to-all-start) | async-done | bytes 262176 | tf_op jit(solution)/shard_map/while/body/eval_jaxpr/all_to_all | solution.py:65
  558.1 22.6 %all-to-all-done = bf16[32,4,8,128]{3,1,2,0:T(4,128)(2,1)S(1)} async-done(((bf16[32,4,8,128]{3,1,2,0:T(4,128)(2,1)}), bf16[32,4,8,128]{3,1,2,0:T(4,128)(2,1)S(1)}, u32[]{:S(2)}, u32[]{:S(2)}) %all-to-all-start) | async-done | bytes 262176 | tf_op jit(solution)/shard_map/while/body/eval_jaxpr/all_to_all | solution.py:65
  583.7 6.0 collective-permute-done
  595.9 22.6 %all-to-all-done = bf16[32,4,8,128]{3,1,2,0:T(4,128)(2,1)S(1)} async-done(((bf16[32,4,8,128]{3,1,2,0:T(4,128)(2,1)}), bf16[32,4,8,128]{3,1,2,0:T(4,128)(2,1)S(1)}, u32[]{:S(2)}, u32[]{:S(2)}) %all-to-all-start) | async-done | bytes 262176 | tf_op jit(solution)/shard_map/while/body/eval_jaxpr/all_to_all | solution.py:65
  621.4 6.0 collective-permute-done
  633.6 22.6 %all-to-all-done = bf16[32,4,8,128]{3,1,2,0:T(4,128)(2,1)S(1)} async-done(((bf16[32,4,8,128]{3,1,2,0:T(4,128)(2,1)}), bf16[32,4,8,128]{3,1,2,0:T(4,128)(2,1)S(1)}, u32[]{:S(2)}, u32[]{:S(2)}) %all-to-all-start) | async-done | bytes 262176 | tf_op jit(solution)/shard_map/while/body/eval_jaxpr/all_to_all | solution.py:65
  671.3 22.6 %all-to-all-done = bf16[32,4,8,128]{3,1,2,0:T(4,128)(2,1)S(1)} async-done(((bf16[32,4,8,128]{3,1,2,0:T(4,128)(2,1)}), bf16[32,4,8,128]{3,1,2,0:T(4,128)(2,1)S(1)}, u32[]{:S(2)}, u32[]{:S(2)}) %all-to-all-start) | async-done | bytes 262176 | tf_op jit(solution)/shard_map/while/body/eval_jaxpr/all_to_all | solution.py:65
  696.9 6.0 collective-permute-done
  709.0 22.6 %all-to-all-done = bf16[32,4,8,128]{3,1,2,0:T(4,128)(2,1)S(1)} async-done(((bf16[32,4,8,128]{3,1,2,0:T(4,128)(2,1)}), bf16[32,4,8,128]{3,1,2,0:T(4,128)(2,1)S(1)}, u32[]{:S(2)}, u32[]{:S(2)}) %all-to-all-start) | async-done | bytes 262176 | tf_op jit(solution)/shard_map/while/body/eval_jaxpr/all_to_all | solution.py:65
  741.3 101.4 %all-reduce.2.cloned.1.call-done = bf16[32,2048]{1,0:T(8,128)(2,1)} async-done(((bf16[32,2048]{1,0:T(8,128)(2,1)}), bf16[32,2048]{1,0:T(8,128)(2,1)}) %all-reduce.2.cloned.1.call-update) | async-done | bytes 131088 | tf_op jit(solution)/shard_map/psum | solution.py:21
  (337 shorter events, 229.8 us)
Async XLA Ops:
  6.5 836.1 %all-reduce.2.cloned.1.call-start = ((), (), s32[]{:S(2)}) async-start(), calls=%async_computation.1 | async-start | bytes 262144 | tf_op jit(solution)/shard_map/psum | solution.py:21
  14.5 38.2 %all-to-all-start = ((bf16[32,4,8,128]{3,1,2,0:T(4,128)(2,1)}), bf16[32,4,8,128]{3,1,2,0:T(4,128)(2,1)S(1)}, u32[]{:S(2)}, u32[]{:S(2)}) async-start(bf16[32,4,8,128]{3,1,2,0:T(4,128)(2,1)} %copy.42), calls=%async_computation | async-start | bytes 524288 | tf_op jit(solution)/shard_map/while/body/eval_jaxpr/all_to_all | solution.py:65
  53.8 7.9 collective-permute-start
  63.8 26.7 %all-to-all-start = ((bf16[32,4,8,128]{3,1,2,0:T(4,128)(2,1)}), bf16[32,4,8,128]{3,1,2,0:T(4,128)(2,1)S(1)}, u32[]{:S(2)}, u32[]{:S(2)}) async-start(bf16[32,4,8,128]{3,1,2,0:T(4,128)(2,1)} %copy.42), calls=%async_computation | async-start | bytes 524288 | tf_op jit(solution)/shard_map/while/body/eval_jaxpr/all_to_all | solution.py:65
  91.5 7.9 collective-permute-start
  101.5 26.7 %all-to-all-start = ((bf16[32,4,8,128]{3,1,2,0:T(4,128)(2,1)}), bf16[32,4,8,128]{3,1,2,0:T(4,128)(2,1)S(1)}, u32[]{:S(2)}, u32[]{:S(2)}) async-start(bf16[32,4,8,128]{3,1,2,0:T(4,128)(2,1)} %copy.42), calls=%async_computation | async-start | bytes 524288 | tf_op jit(solution)/shard_map/while/body/eval_jaxpr/all_to_all | solution.py:65
  129.2 7.9 collective-permute-start
  139.2 26.7 %all-to-all-start = ((bf16[32,4,8,128]{3,1,2,0:T(4,128)(2,1)}), bf16[32,4,8,128]{3,1,2,0:T(4,128)(2,1)S(1)}, u32[]{:S(2)}, u32[]{:S(2)}) async-start(bf16[32,4,8,128]{3,1,2,0:T(4,128)(2,1)} %copy.42), calls=%async_computation | async-start | bytes 524288 | tf_op jit(solution)/shard_map/while/body/eval_jaxpr/all_to_all | solution.py:65
  166.9 7.9 collective-permute-start
  176.9 26.7 %all-to-all-start = ((bf16[32,4,8,128]{3,1,2,0:T(4,128)(2,1)}), bf16[32,4,8,128]{3,1,2,0:T(4,128)(2,1)S(1)}, u32[]{:S(2)}, u32[]{:S(2)}) async-start(bf16[32,4,8,128]{3,1,2,0:T(4,128)(2,1)} %copy.42), calls=%async_computation | async-start | bytes 524288 | tf_op jit(solution)/shard_map/while/body/eval_jaxpr/all_to_all | solution.py:65
  204.7 7.9 collective-permute-start
  214.6 26.7 %all-to-all-start = ((bf16[32,4,8,128]{3,1,2,0:T(4,128)(2,1)}), bf16[32,4,8,128]{3,1,2,0:T(4,128)(2,1)S(1)}, u32[]{:S(2)}, u32[]{:S(2)}) async-start(bf16[32,4,8,128]{3,1,2,0:T(4,128)(2,1)} %copy.42), calls=%async_computation | async-start | bytes 524288 | tf_op jit(solution)/shard_map/while/body/eval_jaxpr/all_to_all | solution.py:65
  242.4 7.9 collective-permute-start
  252.3 26.7 %all-to-all-start = ((bf16[32,4,8,128]{3,1,2,0:T(4,128)(2,1)}), bf16[32,4,8,128]{3,1,2,0:T(4,128)(2,1)S(1)}, u32[]{:S(2)}, u32[]{:S(2)}) async-start(bf16[32,4,8,128]{3,1,2,0:T(4,128)(2,1)} %copy.42), calls=%async_computation | async-start | bytes 524288 | tf_op jit(solution)/shard_map/while/body/eval_jaxpr/all_to_all | solution.py:65
  280.1 7.9 collective-permute-start
  290.0 26.7 %all-to-all-start = ((bf16[32,4,8,128]{3,1,2,0:T(4,128)(2,1)}), bf16[32,4,8,128]{3,1,2,0:T(4,128)(2,1)S(1)}, u32[]{:S(2)}, u32[]{:S(2)}) async-start(bf16[32,4,8,128]{3,1,2,0:T(4,128)(2,1)} %copy.42), calls=%async_computation | async-start | bytes 524288 | tf_op jit(solution)/shard_map/while/body/eval_jaxpr/all_to_all | solution.py:65
  317.8 7.9 collective-permute-start
  327.8 26.7 %all-to-all-start = ((bf16[32,4,8,128]{3,1,2,0:T(4,128)(2,1)}), bf16[32,4,8,128]{3,1,2,0:T(4,128)(2,1)S(1)}, u32[]{:S(2)}, u32[]{:S(2)}) async-start(bf16[32,4,8,128]{3,1,2,0:T(4,128)(2,1)} %copy.42), calls=%async_computation | async-start | bytes 524288 | tf_op jit(solution)/shard_map/while/body/eval_jaxpr/all_to_all | solution.py:65
  355.5 7.9 collective-permute-start
  365.5 26.7 %all-to-all-start = ((bf16[32,4,8,128]{3,1,2,0:T(4,128)(2,1)}), bf16[32,4,8,128]{3,1,2,0:T(4,128)(2,1)S(1)}, u32[]{:S(2)}, u32[]{:S(2)}) async-start(bf16[32,4,8,128]{3,1,2,0:T(4,128)(2,1)} %copy.42), calls=%async_computation | async-start | bytes 524288 | tf_op jit(solution)/shard_map/while/body/eval_jaxpr/all_to_all | solution.py:65
  393.2 7.9 collective-permute-start
  403.2 26.7 %all-to-all-start = ((bf16[32,4,8,128]{3,1,2,0:T(4,128)(2,1)}), bf16[32,4,8,128]{3,1,2,0:T(4,128)(2,1)S(1)}, u32[]{:S(2)}, u32[]{:S(2)}) async-start(bf16[32,4,8,128]{3,1,2,0:T(4,128)(2,1)} %copy.42), calls=%async_computation | async-start | bytes 524288 | tf_op jit(solution)/shard_map/while/body/eval_jaxpr/all_to_all | solution.py:65
  430.9 7.9 collective-permute-start
  440.9 26.7 %all-to-all-start = ((bf16[32,4,8,128]{3,1,2,0:T(4,128)(2,1)}), bf16[32,4,8,128]{3,1,2,0:T(4,128)(2,1)S(1)}, u32[]{:S(2)}, u32[]{:S(2)}) async-start(bf16[32,4,8,128]{3,1,2,0:T(4,128)(2,1)} %copy.42), calls=%async_computation | async-start | bytes 524288 | tf_op jit(solution)/shard_map/while/body/eval_jaxpr/all_to_all | solution.py:65
  478.6 26.7 %all-to-all-start = ((bf16[32,4,8,128]{3,1,2,0:T(4,128)(2,1)}), bf16[32,4,8,128]{3,1,2,0:T(4,128)(2,1)S(1)}, u32[]{:S(2)}, u32[]{:S(2)}) async-start(bf16[32,4,8,128]{3,1,2,0:T(4,128)(2,1)} %copy.42), calls=%async_computation | async-start | bytes 524288 | tf_op jit(solution)/shard_map/while/body/eval_jaxpr/all_to_all | solution.py:65
  516.3 26.7 %all-to-all-start = ((bf16[32,4,8,128]{3,1,2,0:T(4,128)(2,1)}), bf16[32,4,8,128]{3,1,2,0:T(4,128)(2,1)S(1)}, u32[]{:S(2)}, u32[]{:S(2)}) async-start(bf16[32,4,8,128]{3,1,2,0:T(4,128)(2,1)} %copy.42), calls=%async_computation | async-start | bytes 524288 | tf_op jit(solution)/shard_map/while/body/eval_jaxpr/all_to_all | solution.py:65
  554.0 26.7 %all-to-all-start = ((bf16[32,4,8,128]{3,1,2,0:T(4,128)(2,1)}), bf16[32,4,8,128]{3,1,2,0:T(4,128)(2,1)S(1)}, u32[]{:S(2)}, u32[]{:S(2)}) async-start(bf16[32,4,8,128]{3,1,2,0:T(4,128)(2,1)} %copy.42), calls=%async_computation | async-start | bytes 524288 | tf_op jit(solution)/shard_map/while/body/eval_jaxpr/all_to_all | solution.py:65
  591.7 26.7 %all-to-all-start = ((bf16[32,4,8,128]{3,1,2,0:T(4,128)(2,1)}), bf16[32,4,8,128]{3,1,2,0:T(4,128)(2,1)S(1)}, u32[]{:S(2)}, u32[]{:S(2)}) async-start(bf16[32,4,8,128]{3,1,2,0:T(4,128)(2,1)} %copy.42), calls=%async_computation | async-start | bytes 524288 | tf_op jit(solution)/shard_map/while/body/eval_jaxpr/all_to_all | solution.py:65
  619.5 7.9 collective-permute-start
  629.5 26.7 %all-to-all-start = ((bf16[32,4,8,128]{3,1,2,0:T(4,128)(2,1)}), bf16[32,4,8,128]{3,1,2,0:T(4,128)(2,1)S(1)}, u32[]{:S(2)}, u32[]{:S(2)}) async-start(bf16[32,4,8,128]{3,1,2,0:T(4,128)(2,1)} %copy.42), calls=%async_computation | async-start | bytes 524288 | tf_op jit(solution)/shard_map/while/body/eval_jaxpr/all_to_all | solution.py:65
  667.2 26.7 %all-to-all-start = ((bf16[32,4,8,128]{3,1,2,0:T(4,128)(2,1)}), bf16[32,4,8,128]{3,1,2,0:T(4,128)(2,1)S(1)}, u32[]{:S(2)}, u32[]{:S(2)}) async-start(bf16[32,4,8,128]{3,1,2,0:T(4,128)(2,1)} %copy.42), calls=%async_computation | async-start | bytes 524288 | tf_op jit(solution)/shard_map/while/body/eval_jaxpr/all_to_all | solution.py:65
  704.9 26.7 %all-to-all-start = ((bf16[32,4,8,128]{3,1,2,0:T(4,128)(2,1)}), bf16[32,4,8,128]{3,1,2,0:T(4,128)(2,1)S(1)}, u32[]{:S(2)}, u32[]{:S(2)}) async-start(bf16[32,4,8,128]{3,1,2,0:T(4,128)(2,1)} %copy.42), calls=%async_computation | async-start | bytes 524288 | tf_op jit(solution)/shard_map/while/body/eval_jaxpr/all_to_all | solution.py:65
  (45 other events, 1195.6 us)
Sparse Core Ops, SparseCore 0:
  741.4 101.1 all-reduce.1
where the time goes:
time: 854 us; the launch traced here: 851 us
  waiting for transfers between devices  643 us (75%)
  starting transfers between devices  123 us (14%)
  local copies, waits for them, and re-layouts  35.4 us (4%)
  other arithmetic  22 us (3%)
  between operations  13.5 us (2%)
  matrix products  12.4 us (1%)
    all_to_all x19, waiting for transfers between devices, layer(): lax.all_to_all(outgoing, 'width', split_axis=0, concat_axis=0, tiled=True)  429 us
    ppermute x19, waiting for transfers between devices, shifted(): return lax.ppermute(array, axis, pairs)  112 us
    psum x1, waiting for transfers between devices, spread(): return lax.psum(block, axis)  101 us
    all_to_all x19, starting transfers between devices, layer(): lax.all_to_all(outgoing, 'width', split_axis=0, concat_axis=0, tiled=True)  85.1 us
    ppermute x19, starting transfers between devices, shifted(): return lax.ppermute(array, axis, pairs)  38.1 us
    reshape x19, other arithmetic, layer(): pieces = inputs.reshape(BATCH, owned, order)  17.5 us
  transfers between devices with their start and end apart: 39, of which 39 were waited for; matrix products, arithmetic and copies ran while one was open for 0% of the time, Pallas kernels for 0%

commit v1 on v0

v1 whole, which is shorter than its diff:
```python
import functools

import jax
import jax.numpy as jnp
from jax import lax
from jax.experimental import pallas as pl
from jax.experimental.pallas import tpu as pltpu
from jax.sharding import PartitionSpec as P

BATCH = 8
CLIP = 4.0
SLOTS = 2
MESH = pl.DeviceIdType.MESH


def kernel(
    tab_ref, idx_ref, samples_ref, weights_ref, bias_ref, out_ref,
    w, recv, send, stage, act, first, fin, got,
    w_sem, send_sem, recv_sem, fin_sem, got_sem,
):
    segments, shards = lax.axis_size("segment"), lax.axis_size("width")
    seg, me = lax.axis_index("segment"), lax.axis_index("width")
    after = lax.rem(seg + 1, segments)
    before = lax.rem(seg + segments - 1, segments)
    last = segments - 1
    micro, owned, batch, order = first.shape
    per_col = w.shape[1] // order
    share = got.shape[0]
    pairs = batch // share

    load_w = pltpu.make_async_copy(weights_ref, w, w_sem)
    load_w.start()

    barrier = pltpu.get_barrier_semaphore()
    for e in range(shards):
        pl.semaphore_signal(barrier, inc=1, device_id=(before, e), device_id_type=MESH)

    @pl.when(seg != last)
    def _():
        pl.semaphore_signal(barrier, inc=1, device_id=(last, me), device_id_type=MESH)

    pl.semaphore_wait(barrier, jnp.where(seg == last, shards + last, shards))

    offsets = sorted(range(shards), key=lambda o: -min(o, shards - o))

    def emit(m, block):
        for off in offsets:
            d = lax.rem(me + off, shards)
            parts = [block(tab_ref[d * SLOTS + j]) for j in range(SLOTS)]
            send[m, d] = jnp.concatenate(parts, axis=0).astype(jnp.bfloat16)
            pltpu.make_async_remote_copy(
                src_ref=send.at[m, d],
                dst_ref=recv.at[m, me],
                send_sem=send_sem.at[m],
                recv_sem=recv_sem.at[m],
                device_id=(after, d),
                device_id_type=MESH,
            ).start()

    @pl.when(seg == last)
    def _():
        rows = samples_ref.shape[0]
        for c in range(owned):
            block = samples_ref[:, c * order:(c + 1) * order].astype(jnp.float32)
            for m in range(rows // batch):
                first[m, c] = block[m * batch:(m + 1) * batch]

        @pl.loop(0, micro)
        def _(m):
            emit(m, lambda i: first[m, i])

    load_w.wait()

    @pl.loop(0, micro)
    def _(m):
        pltpu.make_async_copy(recv.at[m], recv.at[m], recv_sem.at[m]).wait()
        for e in range(shards):
            both = recv[m, e].astype(jnp.float32)
            for j in range(SLOTS):
                stage[e * SLOTS + j] = both[j * batch:(j + 1) * batch]
        for c in range(owned):
            named = [stage[idx_ref[c * per_col + k]] for k in range(per_col)]
            named = jnp.concatenate(named, axis=1).astype(jnp.bfloat16)
            pre = jnp.dot(named, w[c], preferred_element_type=jnp.float32)
            pre = pre + bias_ref[0:1, c * order:(c + 1) * order]
            act[c] = jnp.clip(pre, 0.0, CLIP)

        @pl.when(seg != last)
        def _():
            emit(m, lambda i: act[i])

        @pl.when(seg == last)
        def _():
            for j in range(pairs):
                for c in range(owned):
                    fin[m, j, :, c * order:(c + 1) * order] = act[
                        c, j * share:(j + 1) * share, :
                    ].astype(jnp.bfloat16)
                owner = m * pairs + j

                @pl.when(owner != last)
                def _():
                    pltpu.make_async_remote_copy(
                        src_ref=fin.at[m, j],
                        dst_ref=got,
                        send_sem=fin_sem,
                        recv_sem=got_sem,
                        device_id=(owner, me),
                        device_id_type=MESH,
                    ).start()

    @pl.loop(0, micro)
    def _(m):
        pltpu.make_async_copy(send.at[m], send.at[m], send_sem.at[m]).wait()

    @pl.when(seg == last)
    def _():
        out_ref[...] = fin[micro - 1, pairs - 1]

        @pl.loop(0, last)
        def _(s):
            pltpu.make_async_copy(fin.at[0, 0], fin.at[0, 0], fin_sem).wait()

    @pl.when(seg != last)
    def _():
        pltpu.make_async_copy(got, got, got_sem).wait()
        out_ref[...] = got[...]


def per_device(samples, occupancy, weights, biases):
    segments, shards = lax.axis_size("segment"), lax.axis_size("width")
    shard = lax.axis_index("width")
    occ = occupancy[0]
    _, owned, per_col, order, _ = weights.shape
    rows, columns = samples.shape
    batch = BATCH
    micro = rows // batch
    share = rows // segments
    requests = owned * per_col

    named = occ.reshape(shards, requests)
    ours = named // owned == shard
    low = jnp.min(jnp.where(ours, named % owned, owned - 1), axis=1)
    high = jnp.max(jnp.where(ours, named % owned, 0), axis=1)
    table = jnp.stack([low, high], axis=1)
    table = lax.ppermute(table, "segment", [(i, (i - 1) % segments) for i in range(segments)])

    mine = lax.dynamic_slice_in_dim(named, shard, 1, 0)[0]
    source = mine // owned
    second = jnp.any(
        (source[:, None] == source[None, :]) & (mine[None, :] < mine[:, None]), axis=1
    )
    index = source * SLOTS + second.astype(jnp.int32)

    smem = pl.BlockSpec(memory_space=pltpu.SMEM)
    vmem = pl.BlockSpec(memory_space=pltpu.VMEM)
    return pl.pallas_call(
        kernel,
        out_shape=jax.ShapeDtypeStruct((share, columns), jnp.bfloat16),
        in_specs=[smem, smem, vmem, pl.BlockSpec(memory_space=pl.ANY), vmem],
        out_specs=vmem,
        scratch_shapes=[
            pltpu.VMEM((owned, per_col * order, order), jnp.bfloat16),
            pltpu.VMEM((micro, shards, SLOTS * batch, order), jnp.bfloat16),
            pltpu.VMEM((micro, shards, SLOTS * batch, order), jnp.bfloat16),
            pltpu.VMEM((shards * SLOTS, batch, order), jnp.float32),
            pltpu.VMEM((owned, batch, order), jnp.float32),
            pltpu.VMEM((micro, owned, batch, order), jnp.float32),
            pltpu.VMEM((micro, batch // share, share, columns), jnp.bfloat16),
            pltpu.VMEM((share, columns), jnp.bfloat16),
            pltpu.SemaphoreType.DMA,
            pltpu.SemaphoreType.DMA((micro,)),
            pltpu.SemaphoreType.DMA((micro,)),
            pltpu.SemaphoreType.DMA,
            pltpu.SemaphoreType.DMA,
        ],
        compiler_params=pltpu.CompilerParams(
            collective_id=0, has_side_effects=True, vmem_limit_bytes=24 * 1024 * 1024
        ),
    )(
        table.reshape(-1), index, samples,
        weights.reshape(owned, per_col * order, order), biases,
    )


def solution(mesh):
    in_specs = (
        P(None, "width"),
        P("segment", None, None),
        P("segment", "width", None, None, None),
        P("segment", "width"),
    )
    return jax.shard_map(
        per_device, mesh=mesh, in_specs=in_specs, out_specs=P("segment", "width"), check_vma=False
    )
```

time: 854 us -> 215 us (0.25)
  waiting for transfers between devices: 643 us -> 0.04 us
  Pallas kernels: 0 us -> 203 us
  starting transfers between devices: 123 us -> 5.19 us
  local copies, waits for them, and re-layouts: 35.4 us -> 5.12 us
  other arithmetic: 22 us -> 1.2 us
  between operations: 13.5 us -> 0.07 us
  matrix products: 12.4 us -> 0 us
    all_to_all x19 -> x0, waiting for transfers between devices: 429 us -> none  [layer(): lax.all_to_all(outgoing, 'width', split_axis=0, concat_axis=0, tiled=True)]
    pallas_call x0 -> x1, Pallas kernels: none -> 203 us  [per_device(): pl.pallas_call(kernel, out_shape=jax.ShapeDtypeStruct((share, columns), j...]
    ppermute x19 -> x1, waiting for transfers between devices: 112 us -> 0.04 us  [per_device(): lax.ppermute(table, 'segment', [(i, (i - 1) % segments) for i in range(se...]
    psum x1 -> x0, waiting for transfers between devices: 101 us -> none  [spread(): return lax.psum(block, axis)]
    all_to_all x19 -> x0, starting transfers between devices: 85.1 us -> none  [layer(): lax.all_to_all(outgoing, 'width', split_axis=0, concat_axis=0, tiled=True)]
    ppermute x19 -> x1, starting transfers between devices: 38.1 us -> 5.19 us  [per_device(): lax.ppermute(table, 'segment', [(i, (i - 1) % segments) for i in range(se...]
    reshape x19 -> x0, other arithmetic: 17.5 us -> none  [layer(): pieces = inputs.reshape(BATCH, owned, order)]
    convert_element_type x19 -> x0, local copies, waits for them, and re-layouts: 15.7 us -> none  [layer(): outgoing = jnp.einsum('drj,bjn->drbn', select, pieces, preferred_element_...]
  transfers between devices with their start and end apart: 39 -> 1, of which waited for: 39 -> 0; matrix products, arithmetic and copies ran while one was open for 0% -> 1% of each run, Pallas kernels for 0% -> 0%
where the time goes in v1:
time: 215 us
  Pallas kernels  203 us (94%)
  starting transfers between devices  5.19 us (2%)
  local copies, waits for them, and re-layouts  5.12 us (2%)
    pallas_call x1, Pallas kernels, per_device(): pl.pallas_call(kernel, out_shape=jax.ShapeDtypeStruct((share, columns), j...  203 us
    ppermute x1, starting transfers between devices, per_device(): lax.ppermute(table, 'segment', [(i, (i - 1) % segments) for i in range(se...  5.19 us
    unnamed x8, local copies, waits for them, and re-layouts  4.63 us
  transfers between devices with their start and end apart: 1, of which 0 were waited for; matrix products, arithmetic and copies ran while one was open for 1% of the time, Pallas kernels for 0%

profile of v1, /device:TPU:6, one launch (start us, length us, event | category | flops | bytes accessed | tf_op | source)
XLA Modules:
  0.0 214.6 jit_solution(8169800101073125131)
XLA Ops:
  0.0 0.7 select_reduce_fusion.1
  0.7 0.1 reduce_min.14
  0.8 0.1 reduce_max.14
  0.9 0.1 reduce_min.18
  1.0 0.1 reduce_max.18
  1.1 5.2 %collective-permute-start = (s32[32,2]{0,1:T(2,128)S(1)}, s32[32,2]{0,1:T(2,128)S(1)}, u32[]{:S(2)}, u32[]{:S(2)}) collective-permute-start(s32[32,2]{0,1:T(2,128)S(1)} %pad_add_fusion), channel_id=1, source_target_pairs={{0,480},{32,0},{64,32},{96,64},{128,96},{160,128},{192,160},{224,1... | collective-permute-start | bytes 776 | tf_op jit(solution)/shard_map/ppermute | solution.py:146
  6.3 0.8 copy.9
  7.2 0.1 reshape_squeeze.3
  7.4 0.2 and_reduce_fusion
  7.6 0.0 collective-permute-done
  7.6 0.1 copy.8
  7.7 0.1 reshape.37.tab_ref
  7.8 0.0 copy-start
  7.8 1.6 copy-done
  9.4 0.0 copy-start.1
  9.4 0.9 copy-done.1
  10.3 0.0 copy-start.2
  10.3 0.7 copy-done.2
  11.0 202.9 %shard_map.46 = bf16[2,2048]{1,0:T(2,128)(2,1)S(1)} custom-call(s32[64]{0:T(128)S(1)} %reshape.37.tab_ref, s32[64]{0:T(128)S(1)} %convert_add_fusion.idx_ref, bf16[32,2048]{1,0:T(8,128)(2,1)S(1)} %copy-done.1, bf16[16,512,128]{2,1,0:T(8,128)(2,1)S(1)} %bitcast.8, f32[1,2048]{1,0:T(1,128)S(1)} %copy-done.2), custom_call_target="tpu_custom_call" | custom-call | tf_op jit(solution)/shard_map/pallas_call | solution.py:157
  214.0 0.6 copy.11
  (4 shorter events, 0.1 us)
Async XLA Ops:
  1.1 6.5 %collective-permute-start = (s32[32,2]{0,1:T(2,128)S(1)}, s32[32,2]{0,1:T(2,128)S(1)}, u32[]{:S(2)}, u32[]{:S(2)}) collective-permute-start(s32[32,2]{0,1:T(2,128)S(1)} %pad_add_fusion), channel_id=1, source_target_pairs={{0,480},{32,0},{64,32},{96,64},{128,96},{160,128},{192,160},{224,1... | collective-permute-start | bytes 776 | tf_op jit(solution)/shard_map/ppermute | solution.py:146
  7.8 1.6 copy-start
  9.4 0.9 copy-start.1
  10.3 0.7 copy-start.2

commit v2 on v1

v2 whole, which is shorter than its diff:
```python
import jax
import jax.numpy as jnp
from jax import lax
from jax.experimental import pallas as pl
from jax.experimental.pallas import tpu as pltpu
from jax.sharding import PartitionSpec as P

BATCH = 4
CLIP = 4.0
SLOTS = 2
LANES = 128
MESH = pl.DeviceIdType.MESH


def kernel(
    occ_ref, samples_ref, weights_ref, bias_ref, out_ref,
    occ, occ_s, own, own_s, table, table_s, index, index_s,
    samples, w, bias, first, send0, send, recv, stage, act, fin, got,
    occ_sem, occ_s_sem, own_sem, table_in_sem, table_out_sem, table_s_sem, index_sem,
    samples_sem, w_sem, bias_sem, send0_sem, send_sem, recv_sem, fin_sem, got_sem,
):
    segments, shards = lax.axis_size("segment"), lax.axis_size("width")
    seg, me = lax.axis_index("segment"), lax.axis_index("width")
    last = segments - 1
    after = lax.rem(seg + 1, segments)
    before = lax.rem(seg + last, segments)
    micro, owned, batch, order = first.shape
    per_col, blocks = occ.shape
    share = got.shape[0]
    pairs = batch // share
    window = index.shape[1]
    offsets = sorted(range(shards), key=lambda o: -min(o, shards - o))

    load_occ = pltpu.make_async_copy(occ_ref, occ, occ_sem)
    load_occ_s = pltpu.make_async_copy(occ_ref, occ_s, occ_s_sem)
    load_w = pltpu.make_async_copy(weights_ref, w, w_sem)
    load_bias = pltpu.make_async_copy(bias_ref, bias, bias_sem)
    load_samples = pltpu.make_async_copy(samples_ref, samples, samples_sem)
    load_occ.start()
    load_occ_s.start()

    barrier = pltpu.get_barrier_semaphore()

    @pl.when(seg > 0)
    def _():
        for off in offsets:
            e = lax.rem(me + off, shards)
            pl.semaphore_signal(barrier, inc=1, device_id=(before, e), device_id_type=MESH)

    @pl.when(seg == 0)
    def _():
        for off in offsets:
            if off:
                e = lax.rem(me + off, shards)
                pl.semaphore_signal(barrier, inc=1, device_id=(seg, e), device_id_type=MESH)
        load_samples.start()

    @pl.when(seg < last)
    def _():
        pl.semaphore_signal(barrier, inc=1, device_id=(after, me), device_id_type=MESH)
        pl.semaphore_signal(barrier, inc=1, device_id=(last, me), device_id_type=MESH)

    load_w.start()
    load_bias.start()

    load_occ.wait()
    named = occ[...]
    ours = named // owned == me
    low = jnp.where(ours, named % owned, owned - 1)
    high = jnp.where(ours, named % owned, 0)
    low_row, high_row = low[0:1], high[0:1]
    for k in range(1, per_col):
        low_row = jnp.minimum(low_row, low[k:k + 1])
        high_row = jnp.maximum(high_row, high[k:k + 1])
    by = 1
    while by < owned:
        low_row = jnp.minimum(low_row, pltpu.roll(low_row, blocks - by, 1))
        high_row = jnp.maximum(high_row, pltpu.roll(high_row, blocks - by, 1))
        by *= 2
    own[0:1] = low_row
    own[1:2] = high_row

    @pl.when(seg == 0)
    def _():
        copy = pltpu.make_async_copy(own, own_s, own_sem)
        copy.start()
        load_samples.wait()
        rows = samples.shape[0]
        for c in range(owned):
            block = samples[:, c * order:(c + 1) * order].astype(jnp.float32)
            for m in range(rows // batch):
                first[m, c] = block[m * batch:(m + 1) * batch]
        copy.wait()

    pl.semaphore_wait(
        barrier,
        jnp.where(seg == last, 1 + last, shards + jnp.where(seg == 0, shards - 1, 1)),
    )

    send_table = pltpu.make_async_remote_copy(
        src_ref=own, dst_ref=table, send_sem=table_out_sem, recv_sem=table_in_sem,
        device_id=(before, me), device_id_type=MESH,
    )

    @pl.when(seg > 0)
    def _():
        send_table.start()

    def emit(m, off, block, tab, out, sem, to):
        d = lax.rem(me + off, shards)
        parts = [block(tab[j, d * owned]) for j in range(SLOTS)]
        out[m, d] = jnp.concatenate(parts, axis=0).astype(jnp.bfloat16)
        if to is None:
            pltpu.make_async_copy(out.at[m, d], recv.at[m, me], recv_sem.at[m]).start()
        else:
            pltpu.make_async_remote_copy(
                src_ref=out.at[m, d], dst_ref=recv.at[m, me],
                send_sem=sem.at[m], recv_sem=recv_sem.at[m],
                device_id=(to, d), device_id_type=MESH,
            ).start()

    @pl.when(seg == 0)
    def _():
        @pl.loop(0, micro)
        def _(m):
            for off in offsets:
                emit(m, off, lambda i: first[m, i], own_s, send0, send0_sem, seg if off else None)

    load_occ_s.wait()
    at = me * owned
    base = at // window * window
    x = occ[:, pl.ds(pl.multiple_of(base, window), window)]
    source = x // owned
    second = jnp.zeros_like(x)
    for k in range(per_col):
        for c in range(owned):
            q = occ_s[k, at + c]
            second = jnp.where((source == q // owned) & (x > q), 1, second)
    index[...] = source * SLOTS + second
    copy_index = pltpu.make_async_copy(index, index_s, index_sem)
    copy_index.start()

    @pl.when(seg < last)
    def _():
        pltpu.make_async_copy(table, table, table_in_sem).wait()
        copy = pltpu.make_async_copy(table, table_s, table_s_sem)
        copy.start()
        copy.wait()

    copy_index.wait()
    load_bias.wait()
    load_w.wait()

    @pl.loop(0, micro)
    def _(m):
        pltpu.make_async_copy(recv.at[m], recv.at[m], recv_sem.at[m]).wait()
        for e in range(shards):
            both = recv[m, e].astype(jnp.float32)
            for j in range(SLOTS):
                stage[e * SLOTS + j] = both[j * batch:(j + 1) * batch]
        for c in range(owned):
            picked = [stage[index_s[k, at - base + c]] for k in range(per_col)]
            picked = jnp.concatenate(picked, axis=1).astype(jnp.bfloat16)
            pre = jnp.dot(picked, w[c], preferred_element_type=jnp.float32)
            pre = pre + bias[0:1, c * order:(c + 1) * order]
            act[c] = jnp.clip(pre, 0.0, CLIP)

        @pl.when(seg < last)
        def _():
            for off in offsets:
                emit(m, off, lambda i: act[i], table_s, send, send_sem, after)

        @pl.when(seg == last)
        def _():
            for j in range(pairs):
                for c in range(owned):
                    fin[m, j, :, c * order:(c + 1) * order] = act[
                        c, j * share:(j + 1) * share, :
                    ].astype(jnp.bfloat16)
                owner = m * pairs + j

                @pl.when(owner != last)
                def _():
                    pltpu.make_async_remote_copy(
                        src_ref=fin.at[m, j], dst_ref=got,
                        send_sem=fin_sem, recv_sem=got_sem,
                        device_id=(owner, me), device_id_type=MESH,
                    ).start()

    @pl.when(seg > 0)
    def _():
        send_table.wait_send()

    @pl.when(seg == 0)
    def _():
        @pl.loop(0, micro)
        def _(m):
            sent = send0.at[m, pl.ds(0, shards - 1)]
            pltpu.make_async_copy(sent, sent, send0_sem.at[m]).wait()

    @pl.when(seg < last)
    def _():
        @pl.loop(0, micro)
        def _(m):
            pltpu.make_async_copy(send.at[m], send.at[m], send_sem.at[m]).wait()

        pltpu.make_async_copy(got, got, got_sem).wait()
        out_ref[...] = got[...]

    @pl.when(seg == last)
    def _():
        out_ref[...] = fin[micro - 1, pairs - 1]

        @pl.loop(0, last)
        def _(s):
            pltpu.make_async_copy(fin.at[0, 0], fin.at[0, 0], fin_sem).wait()


def per_device(samples, occupancy, weights, biases):
    segments, shards = lax.axis_size("segment"), lax.axis_size("width")
    _, owned, per_col, order, _ = weights.shape
    rows, columns = samples.shape
    blocks = occupancy.shape[1]
    batch = BATCH
    micro = rows // batch
    share = rows // segments
    window = min(LANES, blocks)

    hbm = pl.BlockSpec(memory_space=pltpu.HBM)
    slots = (micro, shards, SLOTS * batch, order)
    copies = pltpu.SemaphoreType.DMA
    return pl.pallas_call(
        kernel,
        out_shape=jax.ShapeDtypeStruct((share, columns), jnp.bfloat16),
        in_specs=[hbm] * 4,
        out_specs=pl.BlockSpec(memory_space=pltpu.VMEM),
        scratch_shapes=[
            pltpu.VMEM((per_col, blocks), jnp.int32),
            pltpu.SMEM((per_col, blocks), jnp.int32),
            pltpu.VMEM((SLOTS, blocks), jnp.int32),
            pltpu.SMEM((SLOTS, blocks), jnp.int32),
            pltpu.VMEM((SLOTS, blocks), jnp.int32),
            pltpu.SMEM((SLOTS, blocks), jnp.int32),
            pltpu.VMEM((per_col, window), jnp.int32),
            pltpu.SMEM((per_col, window), jnp.int32),
            pltpu.VMEM((rows, columns), jnp.bfloat16),
            pltpu.VMEM((owned, per_col * order, order), jnp.bfloat16),
            pltpu.VMEM((1, columns), jnp.float32),
            pltpu.VMEM((micro, owned, batch, order), jnp.float32),
            pltpu.VMEM(slots, jnp.bfloat16),
            pltpu.VMEM(slots, jnp.bfloat16),
            pltpu.VMEM(slots, jnp.bfloat16),
            pltpu.VMEM((shards * SLOTS, batch, order), jnp.float32),
            pltpu.VMEM((owned, batch, order), jnp.float32),
            pltpu.VMEM((micro, batch // share, share, columns), jnp.bfloat16),
            pltpu.VMEM((share, columns), jnp.bfloat16),
        ]
        + [copies] * 10
        + [copies((micro,))] * 3
        + [copies] * 2,
        compiler_params=pltpu.CompilerParams(
            collective_id=0, has_side_effects=True, vmem_limit_bytes=60 * 1024 * 1024
        ),
    )(
        jnp.transpose(occupancy[0]), samples,
        weights.reshape(owned, per_col * order, order), biases,
    )


def solution(mesh):
    in_specs = (
        P(None, "width"),
        P("segment", None, None),
        P("segment", "width", None, None, None),
        P("segment", "width"),
    )
    return jax.shard_map(
        per_device, mesh=mesh, in_specs=in_specs, out_specs=P("segment", "width"), check_vma=False
    )
```

time: 215 us -> 186 us (0.87)
  Pallas kernels: 203 us -> 183 us
  starting transfers between devices: 5.19 us -> 0 us
  local copies, waits for them, and re-layouts: 5.12 us -> 1.3 us
    pallas_call x1, Pallas kernels: 203 us -> 183 us  [per_device(): pl.pallas_call(kernel, out_shape=jax.ShapeDtypeStruct((share, columns), j...]
    ppermute x1 -> x0, starting transfers between devices: 5.19 us -> none  [per_device(): lax.ppermute(table, 'segment', [(i, (i - 1) % segments) for i in range(se...]
    unnamed x8 -> x1, local copies, waits for them, and re-layouts: 4.63 us -> 1.3 us
  transfers between devices with their start and end apart: 1 -> 0, of which waited for: 0 -> 0; matrix products, arithmetic and copies ran while one was open for 1% -> 0% of each run, Pallas kernels for 0% -> 0%
where the time goes in v2:
time: 186 us; the launch traced here: 184 us
  Pallas kernels  183 us (98%)
    pallas_call x1, Pallas kernels, per_device(): pl.pallas_call(kernel, out_shape=jax.ShapeDtypeStruct((share, columns), j...  183 us

profile of v2, /device:TPU:6, one launch (start us, length us, event | category | flops | bytes accessed | tf_op | source)
XLA Modules:
  0.0 184.4 jit_solution(263956825725593959)
XLA Ops:
  0.0 183.1 %shard_map.46 = bf16[2,2048]{1,0:T(2,128)(2,1)} custom-call(s32[4,512]{1,0:T(4,128)} %bitcast.5, bf16[32,2048]{1,0:T(8,128)(2,1)} %samples_ref.1, bf16[16,512,128]{2,1,0:T(8,128)(2,1)} %bitcast.4, f32[1,2048]{1,0:T(1,128)} %bias_ref.1), custom_call_target="tpu_custom_call" | custom-call | tf_op jit(solution)/shard_map/pallas_call | solution.py:232
  183.1 1.3 copy.6

commit v3 on v2

--- a/solution.py
+++ b/solution.py
@@ -5,7 +5,7 @@
 from jax.experimental.pallas import tpu as pltpu
 from jax.sharding import PartitionSpec as P
 
-BATCH = 4
+BATCH = 2
 CLIP = 4.0
 SLOTS = 2
 LANES = 128
@@ -14,14 +14,15 @@
 
 def kernel(
     occ_ref, samples_ref, weights_ref, bias_ref, out_ref,
-    occ, occ_s, own, own_s, table, table_s, index, index_s,
+    occ, occ_s, own, table, table_s, first_table, first_table_s, index, index_s,
     samples, w, bias, first, send0, send, recv, stage, act, fin, got,
-    occ_sem, occ_s_sem, own_sem, table_in_sem, table_out_sem, table_s_sem, index_sem,
-    samples_sem, w_sem, bias_sem, send0_sem, send_sem, recv_sem, fin_sem, got_sem,
+    occ_sem, occ_s_sem, table_in_sem, table_out_sem, table_s_sem, first_in_sem, first_s_sem,
+    index_sem, ready_sem, samples_sem, w_sem, bias_sem, send0_sem, send_sem, recv_sem, fin_sem, got_sem,
 ):
     segments, shards = lax.axis_size("segment"), lax.axis_size("width")
     seg, me = lax.axis_index("segment"), lax.axis_index("width")
     last = segments - 1
+    feeder = segments * 3 // 4
     after = lax.rem(seg + 1, segments)
     before = lax.rem(seg + last, segments)
     micro, owned, batch, order = first.shape
@@ -33,7 +34,13 @@
 
     load_occ = pltpu.make_async_copy(occ_ref, occ, occ_sem)
     load_occ_s = pltpu.make_async_copy(occ_ref, occ_s, occ_s_sem)
-    load_w = pltpu.make_async_copy(weights_ref, w, w_sem)
+    half = owned // 2
+    load_w = [
+        pltpu.make_async_copy(
+            weights_ref.at[pl.ds(i * half, half)], w.at[:, :, pl.ds(i * order, order)], w_sem.at[i]
+        )
+        for i in range(2)
+    ]
     load_bias = pltpu.make_async_copy(bias_ref, bias, bias_sem)
     load_samples = pltpu.make_async_copy(samples_ref, samples, samples_sem)
     load_occ.start()
@@ -41,26 +48,27 @@
 
     barrier = pltpu.get_barrier_semaphore()
 
-    @pl.when(seg > 0)
-    def _():
+    def signal_all(semaphore, to):
         for off in offsets:
             e = lax.rem(me + off, shards)
-            pl.semaphore_signal(barrier, inc=1, device_id=(before, e), device_id_type=MESH)
+            pl.semaphore_signal(semaphore, inc=1, device_id=(to, e), device_id_type=MESH)
 
     @pl.when(seg == 0)
     def _():
-        for off in offsets:
-            if off:
-                e = lax.rem(me + off, shards)
-                pl.semaphore_signal(barrier, inc=1, device_id=(seg, e), device_id_type=MESH)
+        signal_all(barrier, feeder)
+
+    @pl.when(seg == feeder)
+    def _():
+        pl.semaphore_signal(barrier, inc=1, device_id=(0, me), device_id_type=MESH)
         load_samples.start()
 
     @pl.when(seg < last)
     def _():
-        pl.semaphore_signal(barrier, inc=1, device_id=(after, me), device_id_type=MESH)
+        signal_all(barrier, after)
         pl.semaphore_signal(barrier, inc=1, device_id=(last, me), device_id_type=MESH)
 
-    load_w.start()
+    for load in load_w:
+        load.start()
     load_bias.start()
 
     load_occ.wait()
@@ -80,51 +88,64 @@
     own[0:1] = low_row
     own[1:2] = high_row
 
-    @pl.when(seg == 0)
-    def _():
-        copy = pltpu.make_async_copy(own, own_s, own_sem)
-        copy.start()
+    @pl.when(seg == feeder)
+    def _():
         load_samples.wait()
         rows = samples.shape[0]
         for c in range(owned):
             block = samples[:, c * order:(c + 1) * order].astype(jnp.float32)
             for m in range(rows // batch):
                 first[m, c] = block[m * batch:(m + 1) * batch]
-        copy.wait()
 
     pl.semaphore_wait(
         barrier,
-        jnp.where(seg == last, 1 + last, shards + jnp.where(seg == 0, shards - 1, 1)),
+        jnp.where(seg == 0, 1, shards)
+        + jnp.where(seg == feeder, shards, 0)
+        + jnp.where(seg == last, last, 0),
     )
 
     send_table = pltpu.make_async_remote_copy(
         src_ref=own, dst_ref=table, send_sem=table_out_sem, recv_sem=table_in_sem,
         device_id=(before, me), device_id_type=MESH,
     )
+    send_first_table = pltpu.make_async_remote_copy(
+        src_ref=own, dst_ref=first_table, send_sem=table_out_sem, recv_sem=first_in_sem,
+        device_id=(feeder, me), device_id_type=MESH,
+    )
+
+    @pl.when(seg == 0)
+    def _():
+        send_first_table.start()
 
     @pl.when(seg > 0)
     def _():
         send_table.start()
 
-    def emit(m, off, block, tab, out, sem, to):
-        d = lax.rem(me + off, shards)
-        parts = [block(tab[j, d * owned]) for j in range(SLOTS)]
-        out[m, d] = jnp.concatenate(parts, axis=0).astype(jnp.bfloat16)
-        if to is None:
-            pltpu.make_async_copy(out.at[m, d], recv.at[m, me], recv_sem.at[m]).start()
-        else:
+    def emit(m, block, tab, out, sem, to):
+        for off in offsets:
+            d = lax.rem(me + off, shards)
+            parts = [block(tab[j, d * owned]) for j in range(SLOTS)]
+            out[m, d] = jnp.concatenate(parts, axis=0).astype(jnp.bfloat16)
             pltpu.make_async_remote_copy(
                 src_ref=out.at[m, d], dst_ref=recv.at[m, me],
                 send_sem=sem.at[m], recv_sem=recv_sem.at[m],
                 device_id=(to, d), device_id_type=MESH,
             ).start()
 
-    @pl.when(seg == 0)
-    def _():
+    @pl.when(seg == feeder)
+    def _():
+        pltpu.make_async_copy(first_table, first_table, first_in_sem).wait()
+        copy = pltpu.make_async_copy(first_table, first_table_s, first_s_sem)
+        copy.start()
+        copy.wait()
+
         @pl.loop(0, micro)
         def _(m):
-            for off in offsets:
-                emit(m, off, lambda i: first[m, i], own_s, send0, send0_sem, seg if off else None)
+            emit(m, lambda i: first[m, i], first_table_s, send0, send0_sem, 0)
+
+    @pl.when(seg > 0)
+    def _():
+        signal_all(ready_sem, before)
 
     load_occ_s.wait()
     at = me * owned
@@ -146,10 +167,12 @@
         copy = pltpu.make_async_copy(table, table_s, table_s_sem)
         copy.start()
         copy.wait()
+        pl.semaphore_wait(ready_sem, shards)
 
     copy_index.wait()
     load_bias.wait()
-    load_w.wait()
+    for load in load_w:
+        load.wait()
 
     @pl.loop(0, micro)
     def _(m):
@@ -158,17 +181,24 @@
             both = recv[m, e].astype(jnp.float32)
             for j in range(SLOTS):
                 stage[e * SLOTS + j] = both[j * batch:(j + 1) * batch]
-        for c in range(owned):
-            picked = [stage[index_s[k, at - base + c]] for k in range(per_col)]
+        for c in range(half):
+            picked = [
+                jnp.concatenate(
+                    [stage[index_s[k, at - base + c + i * half]] for i in range(2)], axis=0
+                )
+                for k in range(per_col)
+            ]
             picked = jnp.concatenate(picked, axis=1).astype(jnp.bfloat16)
             pre = jnp.dot(picked, w[c], preferred_element_type=jnp.float32)
-            pre = pre + bias[0:1, c * order:(c + 1) * order]
-            act[c] = jnp.clip(pre, 0.0, CLIP)
+            for i in range(2):
+                at_c = c + i * half
+                own_pre = pre[i * batch:(i + 1) * batch, i * order:(i + 1) * order]
+                own_pre = own_pre + bias[0:1, at_c * order:(at_c + 1) * order]
+                act[at_c] = jnp.clip(own_pre, 0.0, CLIP)
 
         @pl.when(seg < last)
         def _():
-            for off in offsets:
-                emit(m, off, lambda i: act[i], table_s, send, send_sem, after)
+            emit(m, lambda i: act[i], table_s, send, send_sem, after)
 
         @pl.when(seg == last)
         def _():
@@ -187,16 +217,13 @@
                         device_id=(owner, me), device_id_type=MESH,
                     ).start()
 
-    @pl.when(seg > 0)
-    def _():
-        send_table.wait_send()
-
-    @pl.when(seg == 0)
+    pltpu.make_async_copy(own, own, table_out_sem).wait()
+
+    @pl.when(seg == feeder)
     def _():
         @pl.loop(0, micro)
         def _(m):
-            sent = send0.at[m, pl.ds(0, shards - 1)]
-            pltpu.make_async_copy(sent, sent, send0_sem.at[m]).wait()
+            pltpu.make_async_copy(send0.at[m], send0.at[m], send0_sem.at[m]).wait()
 
     @pl.when(seg < last)
     def _():
@@ -238,13 +265,14 @@
             pltpu.VMEM((per_col, blocks), jnp.int32),
             pltpu.SMEM((per_col, blocks), jnp.int32),
             pltpu.VMEM((SLOTS, blocks), jnp.int32),
+            pltpu.VMEM((SLOTS, blocks), jnp.int32),
             pltpu.SMEM((SLOTS, blocks), jnp.int32),
             pltpu.VMEM((SLOTS, blocks), jnp.int32),
             pltpu.SMEM((SLOTS, blocks), jnp.int32),
             pltpu.VMEM((per_col, window), jnp.int32),
             pltpu.SMEM((per_col, window), jnp.int32),
             pltpu.VMEM((rows, columns), jnp.bfloat16),
-            pltpu.VMEM((owned, per_col * order, order), jnp.bfloat16),
+            pltpu.VMEM((owned // 2, per_col * order, 2 * order), jnp.bfloat16),
             pltpu.VMEM((1, columns), jnp.float32),
             pltpu.VMEM((micro, owned, batch, order), jnp.float32),
             pltpu.VMEM(slots, jnp.bfloat16),
@@ -255,7 +283,9 @@
             pltpu.VMEM((micro, batch // share, share, columns), jnp.bfloat16),
             pltpu.VMEM((share, columns), jnp.bfloat16),
         ]
-        + [copies] * 10
+        + [copies] * 8
+        + [pltpu.SemaphoreType.REGULAR, copies]
+        + [copies((2,)), copies]
         + [copies((micro,))] * 3
         + [copies] * 2,
         compiler_params=pltpu.CompilerParams(

time: 186 us -> 171 us (0.919)
  Pallas kernels: 183 us -> 169 us
    pallas_call x1, Pallas kernels: 183 us -> 169 us  [per_device(): pl.pallas_call(kernel, out_shape=jax.ShapeDtypeStruct((share, columns), j...]
where the time goes in v3:
time: 171 us; the launch traced here: 170 us
  Pallas kernels  169 us (99%)
    pallas_call x1, Pallas kernels, per_device(): pl.pallas_call(kernel, out_shape=jax.ShapeDtypeStruct((share, columns), j...  169 us

profile of v3, /device:TPU:6, one launch (start us, length us, event | category | flops | bytes accessed | tf_op | source)
XLA Modules:
  0.0 170.0 jit_solution(12893761043390058551)
XLA Ops:
  0.0 168.7 %shard_map.46 = bf16[2,2048]{1,0:T(2,128)(2,1)} custom-call(s32[4,512]{1,0:T(4,128)} %bitcast.5, bf16[32,2048]{1,0:T(8,128)(2,1)} %samples_ref.1, bf16[16,512,128]{2,1,0:T(8,128)(2,1)} %bitcast.4, f32[1,2048]{1,0:T(1,128)} %bias_ref.1), custom_call_target="tpu_custom_call" | custom-call | tf_op jit(solution)/shard_map/pallas_call | solution.py:259
  168.7 1.3 copy.6

commit v4 on v3

--- a/solution.py
+++ b/solution.py
@@ -8,15 +8,17 @@
 BATCH = 2
 CLIP = 4.0
 SLOTS = 2
+GROUP = 2
+HEAD = 5
 LANES = 128
 MESH = pl.DeviceIdType.MESH
 
 
 def kernel(
     occ_ref, samples_ref, weights_ref, bias_ref, out_ref,
-    occ, occ_s, own, table, table_s, first_table, first_table_s, index, index_s,
+    occ, occ_s, own, own_s, table, table_s, first_table, first_table_s, index, index_s,
     samples, w, bias, first, send0, send, recv, stage, act, fin, got,
-    occ_sem, occ_s_sem, table_in_sem, table_out_sem, table_s_sem, first_in_sem, first_s_sem,
+    occ_sem, occ_s_sem, own_sem, table_in_sem, table_out_sem, table_s_sem, first_in_sem, first_s_sem,
     index_sem, ready_sem, samples_sem, w_sem, bias_sem, send0_sem, send_sem, recv_sem, fin_sem, got_sem,
 ):
     segments, shards = lax.axis_size("segment"), lax.axis_size("width")
@@ -29,34 +31,34 @@
     per_col, blocks = occ.shape
     share = got.shape[0]
     pairs = batch // share
+    head = min(HEAD, micro)
     window = index.shape[1]
     offsets = sorted(range(shards), key=lambda o: -min(o, shards - o))
 
     load_occ = pltpu.make_async_copy(occ_ref, occ, occ_sem)
     load_occ_s = pltpu.make_async_copy(occ_ref, occ_s, occ_s_sem)
-    half = owned // 2
-    load_w = [
-        pltpu.make_async_copy(
-            weights_ref.at[pl.ds(i * half, half)], w.at[:, :, pl.ds(i * order, order)], w_sem.at[i]
-        )
-        for i in range(2)
-    ]
+    load_w = pltpu.make_async_copy(weights_ref, w, w_sem)
     load_bias = pltpu.make_async_copy(bias_ref, bias, bias_sem)
     load_samples = pltpu.make_async_copy(samples_ref, samples, samples_sem)
+
+    barrier = pltpu.get_barrier_semaphore()
+
+    def signal_all(semaphore, to, others=False):
+        for off in offsets:
+            if others and off == 0:
+                continue
+            e = lax.rem(me + off, shards)
+            pl.semaphore_signal(semaphore, inc=1, device_id=(to, e), device_id_type=MESH)
+
+    @pl.when(seg == 0)
+    def _():
+        signal_all(barrier, seg, others=True)
+        signal_all(barrier, feeder)
+        load_samples.start()
+
     load_occ.start()
     load_occ_s.start()
 
-    barrier = pltpu.get_barrier_semaphore()
-
-    def signal_all(semaphore, to):
-        for off in offsets:
-            e = lax.rem(me + off, shards)
-            pl.semaphore_signal(semaphore, inc=1, device_id=(to, e), device_id_type=MESH)
-
-    @pl.when(seg == 0)
-    def _():
-        signal_all(barrier, feeder)
-
     @pl.when(seg == feeder)
     def _():
         pl.semaphore_signal(barrier, inc=1, device_id=(0, me), device_id_type=MESH)
@@ -67,8 +69,7 @@
         signal_all(barrier, after)
         pl.semaphore_signal(barrier, inc=1, device_id=(last, me), device_id_type=MESH)
 
-    for load in load_w:
-        load.start()
+    load_w.start()
     load_bias.start()
 
     load_occ.wait()
@@ -88,7 +89,11 @@
     own[0:1] = low_row
     own[1:2] = high_row
 
-    @pl.when(seg == feeder)
+    @pl.when(seg == 0)
+    def _():
+        pltpu.make_async_copy(own, own_s, own_sem).start()
+
+    @pl.when((seg == 0) | (seg == feeder))
     def _():
         load_samples.wait()
         rows = samples.shape[0]
@@ -97,9 +102,13 @@
             for m in range(rows // batch):
                 first[m, c] = block[m * batch:(m + 1) * batch]
 
+    @pl.when(seg == 0)
+    def _():
+        pltpu.make_async_copy(own, own_s, own_sem).wait()
+
     pl.semaphore_wait(
         barrier,
-        jnp.where(seg == 0, 1, shards)
+        shards
         + jnp.where(seg == feeder, shards, 0)
         + jnp.where(seg == last, last, 0),
     )
@@ -121,17 +130,26 @@
     def _():
         send_table.start()
 
-    def emit(m, block, tab, out, sem, to):
+    def emit(m, block, tab, out, sem, to, to_self=False):
         for off in offsets:
             d = lax.rem(me + off, shards)
             parts = [block(tab[j, d * owned]) for j in range(SLOTS)]
             out[m, d] = jnp.concatenate(parts, axis=0).astype(jnp.bfloat16)
+            if to_self and off == 0:
+                pltpu.make_async_copy(out.at[m, d], recv.at[m, me], recv_sem.at[m]).start()
+                continue
             pltpu.make_async_remote_copy(
                 src_ref=out.at[m, d], dst_ref=recv.at[m, me],
                 send_sem=sem.at[m], recv_sem=recv_sem.at[m],
                 device_id=(to, d), device_id_type=MESH,
             ).start()
 
+    @pl.when(seg == 0)
+    def _():
+        @pl.loop(0, head)
+        def _(m):
+            emit(m, lambda i: first[m, i], own_s, send0, send0_sem, seg, to_self=True)
+
     @pl.when(seg == feeder)
     def _():
         pltpu.make_async_copy(first_table, first_table, first_in_sem).wait()
@@ -139,7 +157,7 @@
         copy.start()
         copy.wait()
 
-        @pl.loop(0, micro)
+        @pl.loop(head, micro)
         def _(m):
             emit(m, lambda i: first[m, i], first_table_s, send0, send0_sem, 0)
 
@@ -171,8 +189,7 @@
 
     copy_index.wait()
     load_bias.wait()
-    for load in load_w:
-        load.wait()
+    load_w.wait()
 
     @pl.loop(0, micro)
     def _(m):
@@ -181,20 +198,20 @@
             both = recv[m, e].astype(jnp.float32)
             for j in range(SLOTS):
                 stage[e * SLOTS + j] = both[j * batch:(j + 1) * batch]
-        for c in range(half):
+        for c in range(0, owned, GROUP):
             picked = [
                 jnp.concatenate(
-                    [stage[index_s[k, at - base + c + i * half]] for i in range(2)], axis=0
+                    [stage[index_s[k, at - base + c + i]] for i in range(GROUP)], axis=0
                 )
                 for k in range(per_col)
             ]
             picked = jnp.concatenate(picked, axis=1).astype(jnp.bfloat16)
-            pre = jnp.dot(picked, w[c], preferred_element_type=jnp.float32)
-            for i in range(2):
-                at_c = c + i * half
+            wide = jnp.concatenate([w[c + i] for i in range(GROUP)], axis=1)
+            pre = jnp.dot(picked, wide, preferred_element_type=jnp.float32)
+            for i in range(GROUP):
                 own_pre = pre[i * batch:(i + 1) * batch, i * order:(i + 1) * order]
-                own_pre = own_pre + bias[0:1, at_c * order:(at_c + 1) * order]
-                act[at_c] = jnp.clip(own_pre, 0.0, CLIP)
+                own_pre = own_pre + bias[0:1, (c + i) * order:(c + i + 1) * order]
+                act[c + i] = jnp.clip(own_pre, 0.0, CLIP)
 
         @pl.when(seg < last)
         def _():
@@ -219,9 +236,16 @@
 
     pltpu.make_async_copy(own, own, table_out_sem).wait()
 
+    @pl.when(seg == 0)
+    def _():
+        @pl.loop(0, head)
+        def _(m):
+            sent = send0.at[m, pl.ds(0, shards - 1)]
+            pltpu.make_async_copy(sent, sent, send0_sem.at[m]).wait()
+
     @pl.when(seg == feeder)
     def _():
-        @pl.loop(0, micro)
+        @pl.loop(head, micro)
         def _(m):
             pltpu.make_async_copy(send0.at[m], send0.at[m], send0_sem.at[m]).wait()
 
@@ -265,6 +289,7 @@
             pltpu.VMEM((per_col, blocks), jnp.int32),
             pltpu.SMEM((per_col, blocks), jnp.int32),
             pltpu.VMEM((SLOTS, blocks), jnp.int32),
+            pltpu.SMEM((SLOTS, blocks), jnp.int32),
             pltpu.VMEM((SLOTS, blocks), jnp.int32),
             pltpu.SMEM((SLOTS, blocks), jnp.int32),
             pltpu.VMEM((SLOTS, blocks), jnp.int32),
@@ -272,7 +297,7 @@
             pltpu.VMEM((per_col, window), jnp.int32),
             pltpu.SMEM((per_col, window), jnp.int32),
             pltpu.VMEM((rows, columns), jnp.bfloat16),
-            pltpu.VMEM((owned // 2, per_col * order, 2 * order), jnp.bfloat16),
+            pltpu.VMEM((owned, per_col * order, order), jnp.bfloat16),
             pltpu.VMEM((1, columns), jnp.float32),
             pltpu.VMEM((micro, owned, batch, order), jnp.float32),
             pltpu.VMEM(slots, jnp.bfloat16),
@@ -283,9 +308,9 @@
             pltpu.VMEM((micro, batch // share, share, columns), jnp.bfloat16),
             pltpu.VMEM((share, columns), jnp.bfloat16),
         ]
-        + [copies] * 8
+        + [copies] * 9
         + [pltpu.SemaphoreType.REGULAR, copies]
-        + [copies((2,)), copies]
+        + [copies, copies]
         + [copies((micro,))] * 3
         + [copies] * 2,
         compiler_params=pltpu.CompilerParams(

time: 171 us -> 165 us (0.965)
  Pallas kernels: 169 us -> 162 us
    pallas_call x1, Pallas kernels: 169 us -> 162 us  [per_device(): pl.pallas_call(kernel, out_shape=jax.ShapeDtypeStruct((share, columns), j...]
where the time goes in v4:
time: 165 us; the launch traced here: 164 us
  Pallas kernels  162 us (98%)
    pallas_call x1, Pallas kernels, per_device(): pl.pallas_call(kernel, out_shape=jax.ShapeDtypeStruct((share, columns), j...  162 us

profile of v4, /device:TPU:6, one launch (start us, length us, event | category | flops | bytes accessed | tf_op | source)
XLA Modules:
  0.0 163.7 jit_solution(16691478982850873060)
XLA Ops:
  0.0 162.4 %shard_map.46 = bf16[2,2048]{1,0:T(2,128)(2,1)} custom-call(s32[4,512]{1,0:T(4,128)} %bitcast.5, bf16[32,2048]{1,0:T(8,128)(2,1)} %samples_ref.1, bf16[16,512,128]{2,1,0:T(8,128)(2,1)} %bitcast.4, f32[1,2048]{1,0:T(1,128)} %bias_ref.1), custom_call_target="tpu_custom_call" | custom-call | tf_op jit(solution)/shard_map/pallas_call | solution.py:283
  162.4 1.3 copy.6

commit v5 on v4

--- a/solution.py
+++ b/solution.py
@@ -33,6 +33,9 @@
     pairs = batch // share
     head = min(HEAD, micro)
     window = index.shape[1]
+    def around(place):
+        return jnp.where(place >= shards, place - shards, place)
+
     offsets = sorted(range(shards), key=lambda o: -min(o, shards - o))
 
     load_occ = pltpu.make_async_copy(occ_ref, occ, occ_sem)
@@ -47,7 +50,7 @@
         for off in offsets:
             if others and off == 0:
                 continue
-            e = lax.rem(me + off, shards)
+            e = around(me + off)
             pl.semaphore_signal(semaphore, inc=1, device_id=(to, e), device_id_type=MESH)
 
     @pl.when(seg == 0)
@@ -132,7 +135,7 @@
 
     def emit(m, block, tab, out, sem, to, to_self=False):
         for off in offsets:
-            d = lax.rem(me + off, shards)
+            d = around(me + off)
             parts = [block(tab[j, d * owned]) for j in range(SLOTS)]
             out[m, d] = jnp.concatenate(parts, axis=0).astype(jnp.bfloat16)
             if to_self and off == 0:

time: 165 us -> 166 us (level)
  no operation moved by 1% of the time
where the time goes in v5:
time: 166 us; the launch traced here: 164 us
  Pallas kernels  163 us (98%)
    pallas_call x1, Pallas kernels, per_device(): pl.pallas_call(kernel, out_shape=jax.ShapeDtypeStruct((share, columns), j...  163 us

profile of v5, /device:TPU:6, one launch (start us, length us, event | category | flops | bytes accessed | tf_op | source)
XLA Modules:
  0.0 164.3 jit_solution(8700085322938250679)
XLA Ops:
  0.0 163.0 %shard_map.46 = bf16[2,2048]{1,0:T(2,128)(2,1)} custom-call(s32[4,512]{1,0:T(4,128)} %bitcast.5, bf16[32,2048]{1,0:T(8,128)(2,1)} %samples_ref.1, bf16[16,512,128]{2,1,0:T(8,128)(2,1)} %bitcast.4, f32[1,2048]{1,0:T(1,128)} %bias_ref.1), custom_call_target="tpu_custom_call" | custom-call | tf_op jit(solution)/shard_map/pallas_call | solution.py:286
  163.0 1.3 copy.6
